TPU v7x, 256 devices: a whole 4x4x8 slice. The times are simulated.
256 devices in a mesh: pairs: 32 (over y, z), tm: 8 (over x, core).
Axes of the slice: x: 4, y: 4, z: 8, core: 2. Of those that a mesh axis runs over, the one named last changes fastest.
Arguments:
- spectra: bfloat16 [8, 256, 2, 32768], P('tm', 'pairs'), may hold values from -6 to 6
- channel_slot: int32 [256], P('pairs'), may hold values from 0 to 7, as said below
- tile_list: int32 [63, 2], replicated, may hold values from 0 to 31, as said below
- tile_owner: int32 [63], replicated, may hold values from 0 to 31, as said below
Outputs:
- correlations: float32 [128, 64, 256], P('pairs', 'tm')
Inputs may be any that keep to these rules, and one draw needn't show every extreme that they name: `channel_slot`: within each block of 8 channels the values are a permutation of 0..7. `tile_list`: each row (i, j) has j = i or j = i + 1; every such pair of blocks appears exactly once, in some order. `tile_owner`: the owner of the tile in row p of tile_list is that row's i or i + 1; the tile of blocks 0 and 1 is owned by block 1; no owner holds more than 4 tiles, and some owner holds exactly 4.
All inputs are finite; a program needn't handle non-finite values.
Results may differ from a plain program's by a relative error of at most 0.00033.
Values may be sent and summed in bfloat16 or wider, within the bound.
A program may use at most 64 MiB of HBM per device.

v0:
```python
import math

import jax
import jax.numpy as jnp
from jax import lax
from jax.sharding import PartitionSpec as P

LAGS = 256
TILE_CAP = 4


def extended(block, sides, width):
    for axis, dim in sides:
        count = lax.axis_size(axis)
        forward = [(i, i + 1) for i in range(count - 1)]
        backward = [(target, source) for source, target in forward]
        low = lax.ppermute(
            lax.slice_in_dim(block, block.shape[dim] - width, None, axis=dim), axis, forward
        )
        high = lax.ppermute(lax.slice_in_dim(block, 0, width, axis=dim), axis, backward)
        block = jnp.concatenate([low, block, high], axis=dim)
    return block


def lag_table(freq_start, freq_width, bin_count, lag_count):
    freq_ids = freq_start + lax.iota(jnp.int32, freq_width)
    shift_lag = lax.iota(jnp.int32, lag_count) - lag_count // 2
    phase_steps = jnp.mod(freq_ids[:, None] * shift_lag[None, :], 2 * bin_count)
    phase_angle = phase_steps.astype(jnp.float32) * (math.pi / bin_count)
    cosine = jnp.cos(phase_angle).astype(jnp.bfloat16)
    sine_neg = (-jnp.sin(phase_angle)).astype(jnp.bfloat16)
    return jnp.concatenate([cosine, sine_neg], axis=0)


def cross_block(lead_block, tail_block):
    group_count = lead_block.shape[0]
    chan_count = lead_block.shape[1]
    lead_real = lead_block[:, :, 0].astype(jnp.float32)[:, :, None, :]
    lead_imag = lead_block[:, :, 1].astype(jnp.float32)[:, :, None, :]
    tail_real = tail_block[:, :, 0].astype(jnp.float32)[:, None, :, :]
    tail_imag = tail_block[:, :, 1].astype(jnp.float32)[:, None, :, :]
    real_part = lead_real * tail_real + lead_imag * tail_imag
    imag_part = lead_imag * tail_real - lead_real * tail_imag
    joined = jnp.concatenate(
        [real_part.astype(jnp.bfloat16), imag_part.astype(jnp.bfloat16)], axis=-1
    )
    return joined.reshape(group_count, chan_count * chan_count, joined.shape[-1])


def correlate(blocks, lead_pos, tail_pos, norm_scale):
    chan_count = blocks.shape[1]
    bin_count = blocks.shape[3]
    freq_width = min(2048, bin_count)
    slot_count = lead_pos.shape[0]

    def freq_turn(step_index, running):
        freq_start = step_index * freq_width
        freq_piece = lax.dynamic_slice_in_dim(blocks, freq_start, freq_width, 3)
        lead_block = jnp.take(freq_piece, lead_pos, axis=0)
        tail_block = jnp.take(freq_piece, tail_pos, axis=0)
        cross_spec = cross_block(lead_block, tail_block)
        lag_rows = lag_table(freq_start, freq_width, bin_count, LAGS)
        return running + jnp.einsum(
            "spf,fl->spl", cross_spec, lag_rows, preferred_element_type=jnp.float32
        )

    start_sum = jnp.zeros((slot_count, chan_count * chan_count, LAGS), jnp.float32)
    running = lax.fori_loop(0, bin_count // freq_width, freq_turn, start_sum)
    return running * norm_scale


def stack_windows(window_terms):
    summed = lax.psum(window_terms, "tm")
    share_rows = summed.shape[1] // lax.axis_size("tm")
    return lax.dynamic_slice_in_dim(summed, lax.axis_index("tm") * share_rows, share_rows, 1)


def on_device(spectra, channel_slot, tile_list, tile_owner):
    here_index = lax.axis_index("pairs")
    bin_count = spectra.shape[3]
    norm_scale = 1.0 / math.sqrt(2.0 * bin_count * lax.axis_size("tm"))
    ordered = jnp.take(spectra[0], channel_slot, axis=0)
    chan_count = ordered.shape[0]
    tile_count = tile_list.shape[0]
    low_block = tile_list[:, 0]
    high_block = tile_list[:, 1]
    earlier = lax.iota(jnp.int32, tile_count)[:, None] > lax.iota(jnp.int32, tile_count)[None, :]
    slot_rank = jnp.sum((tile_owner[:, None] == tile_owner[None, :]) & earlier, axis=1)
    slot_ids = lax.iota(jnp.int32, TILE_CAP)
    owned_slot = (
        (tile_owner[None, :] == here_index) & (slot_rank[None, :] == slot_ids[:, None])
    ).astype(jnp.int32)
    live_slot = jnp.sum(owned_slot, axis=1)
    slot_low = jnp.sum(owned_slot * low_block[None, :], axis=1)
    slot_high = jnp.sum(owned_slot * high_block[None, :], axis=1)
    widened = extended(ordered, (("pairs", 0),), chan_count)
    blocks = widened.reshape(3, chan_count, widened.shape[1], widened.shape[2])
    lead_pos = jnp.clip(slot_low - here_index + 1, 0, 2)
    tail_pos = jnp.clip(slot_high - here_index + 1, 0, 2)
    window_terms = correlate(blocks, lead_pos, tail_pos, norm_scale)
    window_terms = window_terms * live_slot[:, None, None].astype(jnp.float32)
    return stack_windows(window_terms)


def solution(mesh):
    placed = (P("tm", "pairs", None, None), P("pairs"), P(), P())
    return jax.shard_map(
        on_device, mesh=mesh, in_specs=placed, out_specs=P("pairs", "tm", None), check_vma=False
    )
```

profile of v0, /device:TPU:24, one launch (start us, length us, event | category | flops | bytes accessed | tf_op | source)
XLA Modules:
  0.0 379.6 jit_solution(1595996826397353993)
XLA Ops:
  8.0 2.7 gather_fusion.2
  11.6 7.9 %collective-permute-start.1 = (bf16[8,2,32768]{2,1,0:T(2,128)(2,1)S(1)}, bf16[8,2,32768]{2,1,0:T(2,128)(2,1)S(1)}, u32[]{:S(2)}, u32[]{:S(2)}) collective-permute-start(bf16[8,2,32768]{2,1,0:T(2,128)(2,1)S(1)} %broadcast_select_fusion.2), channel_id=1, source_target_pairs={{8,0},{16,8},{24,16},{32,24},{40,32},{48,40},{56,48},{64,56},{72,6... | collective-permute-start | bytes 3145736 | tf_op jit(solution)/shard_map/ppermute | solution.py:20
  19.6 1.9 collective-permute-start
  21.9 20.1 %collective-permute-done.1 = bf16[8,2,32768]{2,1,0:T(2,128)(2,1)S(1)} collective-permute-done((bf16[8,2,32768]{2,1,0:T(2,128)(2,1)S(1)}, bf16[8,2,32768]{2,1,0:T(2,128)(2,1)S(1)}, u32[]{:S(2)}, u32[]{:S(2)}) %collective-permute-start.1) | collective-permute-done | bytes 1048608 | tf_op jit(solution)/shard_map/ppermute | solution.py:20
  42.0 6.3 %collective-permute-done = bf16[8,2,32768]{2,1,0:T(2,128)(2,1)} collective-permute-done((bf16[8,2,32768]{2,1,0:T(2,128)(2,1)S(1)}, bf16[8,2,32768]{2,1,0:T(2,128)(2,1)}, u32[]{:S(2)}, u32[]{:S(2)}) %collective-permute-start) | collective-permute-done | bytes 1048608 | tf_op jit(solution)/shard_map/ppermute | solution.py:17
  48.3 7.1 %pad_maximum_fusion = bf16[24,2,32768]{2,1,0:T(2,128)(2,1)} fusion(bf16[8,2,32768]{2,1,0:T(2,128)(2,1)S(1)} %collective-permute-done.1, bf16[8,2,32768]{2,1,0:T(2,128)(2,1)S(1)} %broadcast_select_fusion.2, bf16[8,2,32768]{2,1,0:T(2,128)(2,1)} %collective-permute-done), kind=kLoop, calls=%fused_computation.45 | loop fusion | flops 3145728 | bytes 6291456 | tf_op jit(solution)/shard_map/concatenate | solution.py:21
  55.4 254.1 %while.16 = (s32[]{:T(128)}, f32[4,64,256]{2,1,0:T(8,128)S(1)}, bf16[3,8,2,32768]{3,2,1,0:T(2,128)(2,1)}, s32[4]{0:T(128)S(1)}, s32[4]{0:T(128)S(1)}, /*index=5*/s32[]{:T(128)}, s32[]{:T(128)}, s32[]{:T(128)}, s32[]{:T(128)}) while((s32[]{:T(128)}, f32[4,64,256]{2,1,0:T(8,128)S(1)}, bf16[3,8,2,32768]{3,2,1,0:T(2,128)(2,1)}, ...), condition=%wide.region_4.6_spmd.clone, body=%wide.region_3.5_spmd.clone.sunk | while | flops 559026496 | bytes 16148821 | solution.py:68
  55.5 1.1 constant_dynamic-slice_fusion.3
  56.6 1.1 gather_fusion.1
  57.9 1.1 gather_fusion
  61.0 9.4 %cosine_convert_fusion.2 = (bf16[2048,256]{1,0:T(8,128)(2,1)S(1)}, bf16[2048,256]{1,0:T(8,128)(2,1)S(1)}) fusion(s32[256]{0:T(256)S(1)} %iota_add_fusion.4, s32[2048]{0:T(1024)S(1)} %iota_add_fusion.5), kind=kLoop, calls=%fused_computation.19.clone.1 | loop fusion | flops 8912896 | bytes 2106368 | tf_op jit(solution)/shard_map/while/body/eval_jaxpr/convert_element_type | solution.py:30
  71.4 1.1 constant_dynamic-slice_fusion.3
  72.5 1.1 gather_fusion.1
  73.8 1.1 gather_fusion
  76.9 9.4 %cosine_convert_fusion.2 = (bf16[2048,256]{1,0:T(8,128)(2,1)S(1)}, bf16[2048,256]{1,0:T(8,128)(2,1)S(1)}) fusion(s32[256]{0:T(256)S(1)} %iota_add_fusion.4, s32[2048]{0:T(1024)S(1)} %iota_add_fusion.5), kind=kLoop, calls=%fused_computation.19.clone.1 | loop fusion | flops 8912896 | bytes 2106368 | tf_op jit(solution)/shard_map/while/body/eval_jaxpr/convert_element_type | solution.py:30
  87.3 1.1 constant_dynamic-slice_fusion.3
  88.3 1.1 gather_fusion.1
  89.7 1.1 gather_fusion
  92.8 9.4 %cosine_convert_fusion.2 = (bf16[2048,256]{1,0:T(8,128)(2,1)S(1)}, bf16[2048,256]{1,0:T(8,128)(2,1)S(1)}) fusion(s32[256]{0:T(256)S(1)} %iota_add_fusion.4, s32[2048]{0:T(1024)S(1)} %iota_add_fusion.5), kind=kLoop, calls=%fused_computation.19.clone.1 | loop fusion | flops 8912896 | bytes 2106368 | tf_op jit(solution)/shard_map/while/body/eval_jaxpr/convert_element_type | solution.py:30
  104.2 1.1 gather_fusion.1
  105.6 1.1 gather_fusion
  108.7 9.4 %cosine_convert_fusion.2 = (bf16[2048,256]{1,0:T(8,128)(2,1)S(1)}, bf16[2048,256]{1,0:T(8,128)(2,1)S(1)}) fusion(s32[256]{0:T(256)S(1)} %iota_add_fusion.4, s32[2048]{0:T(1024)S(1)} %iota_add_fusion.5), kind=kLoop, calls=%fused_computation.19.clone.1 | loop fusion | flops 8912896 | bytes 2106368 | tf_op jit(solution)/shard_map/while/body/eval_jaxpr/convert_element_type | solution.py:30
  120.1 1.1 gather_fusion.1
  121.5 1.1 gather_fusion
  124.6 9.4 %cosine_convert_fusion.2 = (bf16[2048,256]{1,0:T(8,128)(2,1)S(1)}, bf16[2048,256]{1,0:T(8,128)(2,1)S(1)}) fusion(s32[256]{0:T(256)S(1)} %iota_add_fusion.4, s32[2048]{0:T(1024)S(1)} %iota_add_fusion.5), kind=kLoop, calls=%fused_computation.19.clone.1 | loop fusion | flops 8912896 | bytes 2106368 | tf_op jit(solution)/shard_map/while/body/eval_jaxpr/convert_element_type | solution.py:30
  134.9 1.1 constant_dynamic-slice_fusion.3
  136.0 1.1 gather_fusion.1
  137.4 1.1 gather_fusion
  140.4 9.4 %cosine_convert_fusion.2 = (bf16[2048,256]{1,0:T(8,128)(2,1)S(1)}, bf16[2048,256]{1,0:T(8,128)(2,1)S(1)}) fusion(s32[256]{0:T(256)S(1)} %iota_add_fusion.4, s32[2048]{0:T(1024)S(1)} %iota_add_fusion.5), kind=kLoop, calls=%fused_computation.19.clone.1 | loop fusion | flops 8912896 | bytes 2106368 | tf_op jit(solution)/shard_map/while/body/eval_jaxpr/convert_element_type | solution.py:30
  150.8 1.1 constant_dynamic-slice_fusion.3
  151.9 1.1 gather_fusion.1
  153.2 1.1 gather_fusion
  156.3 9.4 %cosine_convert_fusion.2 = (bf16[2048,256]{1,0:T(8,128)(2,1)S(1)}, bf16[2048,256]{1,0:T(8,128)(2,1)S(1)}) fusion(s32[256]{0:T(256)S(1)} %iota_add_fusion.4, s32[2048]{0:T(1024)S(1)} %iota_add_fusion.5), kind=kLoop, calls=%fused_computation.19.clone.1 | loop fusion | flops 8912896 | bytes 2106368 | tf_op jit(solution)/shard_map/while/body/eval_jaxpr/convert_element_type | solution.py:30
  166.7 1.1 constant_dynamic-slice_fusion.3
  167.7 1.1 gather_fusion.1
  169.1 1.1 gather_fusion
  172.2 9.4 %cosine_convert_fusion.2 = (bf16[2048,256]{1,0:T(8,128)(2,1)S(1)}, bf16[2048,256]{1,0:T(8,128)(2,1)S(1)}) fusion(s32[256]{0:T(256)S(1)} %iota_add_fusion.4, s32[2048]{0:T(1024)S(1)} %iota_add_fusion.5), kind=kLoop, calls=%fused_computation.19.clone.1 | loop fusion | flops 8912896 | bytes 2106368 | tf_op jit(solution)/shard_map/while/body/eval_jaxpr/convert_element_type | solution.py:30
  183.6 1.1 gather_fusion.1
  185.0 1.1 gather_fusion
  188.1 9.4 %cosine_convert_fusion.2 = (bf16[2048,256]{1,0:T(8,128)(2,1)S(1)}, bf16[2048,256]{1,0:T(8,128)(2,1)S(1)}) fusion(s32[256]{0:T(256)S(1)} %iota_add_fusion.4, s32[2048]{0:T(1024)S(1)} %iota_add_fusion.5), kind=kLoop, calls=%fused_computation.19.clone.1 | loop fusion | flops 8912896 | bytes 2106368 | tf_op jit(solution)/shard_map/while/body/eval_jaxpr/convert_element_type | solution.py:30
  198.4 1.1 constant_dynamic-slice_fusion.3
  199.5 1.1 gather_fusion.1
  200.9 1.1 gather_fusion
  204.0 9.4 %cosine_convert_fusion.2 = (bf16[2048,256]{1,0:T(8,128)(2,1)S(1)}, bf16[2048,256]{1,0:T(8,128)(2,1)S(1)}) fusion(s32[256]{0:T(256)S(1)} %iota_add_fusion.4, s32[2048]{0:T(1024)S(1)} %iota_add_fusion.5), kind=kLoop, calls=%fused_computation.19.clone.1 | loop fusion | flops 8912896 | bytes 2106368 | tf_op jit(solution)/shard_map/while/body/eval_jaxpr/convert_element_type | solution.py:30
  215.4 1.1 gather_fusion.1
  216.8 1.1 gather_fusion
  219.8 9.4 %cosine_convert_fusion.2 = (bf16[2048,256]{1,0:T(8,128)(2,1)S(1)}, bf16[2048,256]{1,0:T(8,128)(2,1)S(1)}) fusion(s32[256]{0:T(256)S(1)} %iota_add_fusion.4, s32[2048]{0:T(1024)S(1)} %iota_add_fusion.5), kind=kLoop, calls=%fused_computation.19.clone.1 | loop fusion | flops 8912896 | bytes 2106368 | tf_op jit(solution)/shard_map/while/body/eval_jaxpr/convert_element_type | solution.py:30
  231.3 1.1 gather_fusion.1
  232.7 1.1 gather_fusion
  235.7 9.4 %cosine_convert_fusion.2 = (bf16[2048,256]{1,0:T(8,128)(2,1)S(1)}, bf16[2048,256]{1,0:T(8,128)(2,1)S(1)}) fusion(s32[256]{0:T(256)S(1)} %iota_add_fusion.4, s32[2048]{0:T(1024)S(1)} %iota_add_fusion.5), kind=kLoop, calls=%fused_computation.19.clone.1 | loop fusion | flops 8912896 | bytes 2106368 | tf_op jit(solution)/shard_map/while/body/eval_jaxpr/convert_element_type | solution.py:30
  247.2 1.1 gather_fusion.1
  248.5 1.1 gather_fusion
  251.6 9.4 %cosine_convert_fusion.2 = (bf16[2048,256]{1,0:T(8,128)(2,1)S(1)}, bf16[2048,256]{1,0:T(8,128)(2,1)S(1)}) fusion(s32[256]{0:T(256)S(1)} %iota_add_fusion.4, s32[2048]{0:T(1024)S(1)} %iota_add_fusion.5), kind=kLoop, calls=%fused_computation.19.clone.1 | loop fusion | flops 8912896 | bytes 2106368 | tf_op jit(solution)/shard_map/while/body/eval_jaxpr/convert_element_type | solution.py:30
  263.0 1.1 gather_fusion.1
  264.4 1.1 gather_fusion
  267.5 9.4 %cosine_convert_fusion.2 = (bf16[2048,256]{1,0:T(8,128)(2,1)S(1)}, bf16[2048,256]{1,0:T(8,128)(2,1)S(1)}) fusion(s32[256]{0:T(256)S(1)} %iota_add_fusion.4, s32[2048]{0:T(1024)S(1)} %iota_add_fusion.5), kind=kLoop, calls=%fused_computation.19.clone.1 | loop fusion | flops 8912896 | bytes 2106368 | tf_op jit(solution)/shard_map/while/body/eval_jaxpr/convert_element_type | solution.py:30
  278.9 1.1 gather_fusion.1
  280.3 1.1 gather_fusion
  283.4 9.4 %cosine_convert_fusion.2 = (bf16[2048,256]{1,0:T(8,128)(2,1)S(1)}, bf16[2048,256]{1,0:T(8,128)(2,1)S(1)}) fusion(s32[256]{0:T(256)S(1)} %iota_add_fusion.4, s32[2048]{0:T(1024)S(1)} %iota_add_fusion.5), kind=kLoop, calls=%fused_computation.19.clone.1 | loop fusion | flops 8912896 | bytes 2106368 | tf_op jit(solution)/shard_map/while/body/eval_jaxpr/convert_element_type | solution.py:30
  294.8 1.1 gather_fusion.1
  296.2 1.1 gather_fusion
  299.3 9.4 %cosine_convert_fusion.2 = (bf16[2048,256]{1,0:T(8,128)(2,1)S(1)}, bf16[2048,256]{1,0:T(8,128)(2,1)S(1)}) fusion(s32[256]{0:T(256)S(1)} %iota_add_fusion.4, s32[2048]{0:T(1024)S(1)} %iota_add_fusion.5), kind=kLoop, calls=%fused_computation.19.clone.1 | loop fusion | flops 8912896 | bytes 2106368 | tf_op jit(solution)/shard_map/while/body/eval_jaxpr/convert_element_type | solution.py:30
  310.3 61.1 %all-reduce.2.cloned.1.call-done = f32[4,64,256]{2,1,0:T(8,128)} async-done(((f32[4,64,256]{2,1,0:T(8,128)}), f32[4,64,256]{2,1,0:T(8,128)}) %all-reduce.2.cloned.1.call-update) | async-done | bytes 262160 | tf_op jit(solution)/shard_map/psum | solution.py:73
  371.4 1.4 constant_dynamic-slice_fusion.1
  (285 shorter events, 62.3 us)
Async XLA Ops:
  6.5 1.4 copy-start
  6.5 364.9 %all-reduce.2.cloned.1.call-start = ((), (), s32[]{:S(2)}) async-start(), calls=%async_computation | async-start | bytes 524288 | tf_op jit(solution)/shard_map/psum | solution.py:73
  8.0 13.5 %copy-start.2 = (s32[63]{0:T(128)S(1)}, s32[63]{0:T(128)}, u32[]{:S(2)}) copy-start(s32[63]{0:T(128)} %param.11) | copy-start | bytes 760
  8.0 13.8 %copy-start.1 = (s32[63,2]{0,1:T(2,128)S(1)}, s32[63,2]{0,1:T(2,128)}, u32[]{:S(2)}) copy-start(s32[63,2]{0,1:T(2,128)} %param.10) | copy-start | bytes 1516
  11.6 30.3 %collective-permute-start.1 = (bf16[8,2,32768]{2,1,0:T(2,128)(2,1)S(1)}, bf16[8,2,32768]{2,1,0:T(2,128)(2,1)S(1)}, u32[]{:S(2)}, u32[]{:S(2)}) collective-permute-start(bf16[8,2,32768]{2,1,0:T(2,128)(2,1)S(1)} %broadcast_select_fusion.2), channel_id=1, source_target_pairs={{8,0},{16,8},{24,16},{32,24},{40,32},{48,40},{56,48},{64,56},{72,6... | collective-permute-start | bytes 3145736 | tf_op jit(solution)/shard_map/ppermute | solution.py:20
  19.6 28.7 %collective-permute-start = (bf16[8,2,32768]{2,1,0:T(2,128)(2,1)S(1)}, bf16[8,2,32768]{2,1,0:T(2,128)(2,1)}, u32[]{:S(2)}, u32[]{:S(2)}) collective-permute-start(bf16[8,2,32768]{2,1,0:T(2,128)(2,1)S(1)} %broadcast_select_fusion.2), channel_id=1, source_target_pairs={{0,8},{8,16},{16,24},{24,32},{32,40},{40,48},{48,56},{56,64},{64,7... | collective-permute-start | bytes 3145736 | tf_op jit(solution)/shard_map/ppermute | solution.py:17
Sparse Core Ops, SparseCore 0:
  310.4 60.9 all-reduce.1
where the time goes:
time: 381 us; the launch traced here: 380 us
  other arithmetic  192 us (50%)
  waiting for transfers between devices  87.5 us (23%)
  local copies, waits for them, and re-layouts  60.9 us (16%)
  between operations  13.5 us (4%)
  matrix products  12.9 us (3%)
  starting transfers between devices  9.87 us (3%)
    convert_element_type x16, other arithmetic, lag_table(): cosine = jnp.cos(phase_angle).astype(jnp.bfloat16)  151 us
    psum x1, waiting for transfers between devices, stack_windows(): summed = lax.psum(window_terms, 'tm')  61.1 us
    ppermute x1, waiting for transfers between devices, extended(): lax.ppermute(lax.slice_in_dim(block, 0, width, axis=dim), axis, backward)  20.1 us
    gather x16, local copies, waits for them, and re-layouts, freq_turn(): tail_block = jnp.take(freq_piece, tail_pos, axis=0)  17.2 us
    gather x16, local copies, waits for them, and re-layouts, freq_turn(): lead_block = jnp.take(freq_piece, lead_pos, axis=0)  17.2 us
    dynamic_slice x16, local copies, waits for them, and re-layouts, freq_turn(): freq_piece = lax.dynamic_slice_in_dim(blocks, freq_start, freq_width, 3)  17.1 us
    dot_general x16, matrix products, freq_turn(): jnp.einsum('spf,fl->spl', cross_spec, lag_rows, preferred_element_type=jn...  12.9 us
    convert_element_type x16, other arithmetic, cross_block(): real_part.astype(jnp.bfloat16)  8.57 us
  transfers between devices with their start and end apart: 3, of which 3 were waited for; matrix products, arithmetic and copies ran while one was open for 0% of the time, Pallas kernels for 0%

commit v1 on v0

v1 whole, which is shorter than its diff:
```python
import functools
import math

import jax
import jax.numpy as jnp
import ml_dtypes
import numpy as np
from jax import lax
from jax.experimental import pallas as pl
from jax.experimental.pallas import tpu as pltpu
from jax.sharding import PartitionSpec as P

LAGS = 256
TILE_CAP = 4
CH = 8
HALF = LAGS // 2
TURN = 512
SHIFT = TURN // 4
STEP = 4096
MESH = pl.DeviceIdType.MESH
F32 = jnp.float32
BF16 = jnp.bfloat16


def lag_table(bins):
    bin_ids = np.arange(bins)
    turn_start = bin_ids // TURN * TURN
    moved = turn_start + (bin_ids - turn_start + SHIFT) % TURN

    def phase(ids, lags):
        steps = (ids[:, None] * lags[None, :]) % (2 * bins)
        return (steps.astype(np.float32) * np.float32(math.pi / bins)).astype(np.float64)

    cosine = np.cos(phase(bin_ids, np.arange(HALF)))
    sine = -np.sin(phase(moved, np.arange(HALF)))
    sine[:, :1] = np.cos(phase(bin_ids, np.array([HALF])))
    joined = np.concatenate([cosine, sine], axis=1)
    return joined.astype(np.float32).astype(ml_dtypes.bfloat16)


def moved_on(block):
    parts = []
    for start in range(0, block.shape[1], TURN):
        parts.append(block[:, start + SHIFT : start + TURN])
        parts.append(block[:, start : start + SHIFT])
    return jnp.concatenate(parts, axis=1)


def cross_rows(lead, tail):
    lead = lead.astype(F32)
    tail = tail.astype(F32)
    tail_re, tail_im = tail[:CH], tail[CH:]
    real, imag = [], []
    for a in range(CH):
        lead_re, lead_im = lead[a : a + 1], lead[CH + a : CH + a + 1]
        real.append(lead_re * tail_re + lead_im * tail_im)
        imag.append(lead_im * tail_re - lead_re * tail_im)
    real = jnp.concatenate(real, axis=0).astype(BF16)
    imag = jnp.concatenate(imag, axis=0).astype(BF16)
    return jnp.concatenate([real, moved_on(imag)], axis=0)


def folded(acc):
    real, imag = acc[: CH * CH, :], acc[CH * CH :, :]
    lane = lax.broadcasted_iota(jnp.int32, (CH * CH, HALF), 1)
    right = imag[:, HALF:] + jnp.where(lane == 0, real[:, HALF:], 0.0)
    return jnp.concatenate([real[:, :HALF], right], axis=1)


def kernel(
    n_pairs, n_tm, norm_scale,
    spectra, slot_hbm, tiles_hbm, owners_hbm, table_hbm,
    out,
    slot, tiles, owners, raw, own, from_right, from_left, table,
    diag_acc, low_acc, high_acc,
    diag_out, diag_in, side_out, side_in, hop_out, hop_in,
    index_sem, raw_sem, table_sem, send_sem, recv_sem, diag_send, diag_recv,
    side_send, side_recv, hop_send, hop_recv,
):
    bins = own.shape[1]
    half_bins = bins // 2
    steps = half_bins // STEP
    here = lax.axis_index("pairs")
    window = lax.axis_index("tm")
    right = (lax.rem(here + 1, n_pairs), window)
    left = (lax.rem(here + n_pairs - 1, n_pairs), window)

    def peer(k):
        return lax.rem(window + k, n_tm)

    barrier = pltpu.get_barrier_semaphore()
    for device in [right, left] + [(here, peer(k)) for k in range(1, n_tm)]:
        pl.semaphore_signal(barrier, inc=1, device_id=device, device_id_type=MESH)

    def lanes(index):
        return pl.ds(pl.multiple_of(index * STEP, STEP), STEP)

    order = [part for i in range(steps) for part in (i, steps + i)]

    def raw_copy(part):
        return pltpu.make_async_copy(
            spectra.at[:, :, lanes(part)], raw[part], raw_sem.at[part]
        )

    def table_copy(part):
        return pltpu.make_async_copy(
            table_hbm.at[lanes(part), :], table.at[lanes(part), :], table_sem.at[part]
        )

    index_copies = [
        pltpu.make_async_copy(source, target, index_sem.at[place])
        for place, (source, target) in enumerate(
            [(slot_hbm, slot), (tiles_hbm, tiles), (owners_hbm, owners)]
        )
    ]
    index_copies[0].start()
    for part in order:
        raw_copy(part).start()
    for copy in index_copies[1:]:
        copy.start()
    for part in range(2 * steps):
        table_copy(part).start()

    def low_copy(i):
        return pltpu.make_async_remote_copy(
            own.at[:, lanes(i)], from_right.at[:, lanes(i)],
            send_sem.at[i], recv_sem.at[i], device_id=left, device_id_type=MESH,
        )

    def high_copy(i):
        return pltpu.make_async_remote_copy(
            own.at[:, lanes(steps + i)], from_left.at[:, lanes(i)],
            send_sem.at[steps + i], recv_sem.at[steps + i],
            device_id=right, device_id_type=MESH,
        )

    def send(part):
        if part < steps:
            low_copy(part).start()
        else:
            high_copy(part - steps).start()

    index_copies[0].wait()
    rows = [slot[c] for c in range(CH)]
    for place, part in enumerate(order):
        raw_copy(part).wait()

        @pl.loop(0, STEP // 1024)
        def _(piece, part=part):
            offset = pl.multiple_of(piece * 1024, 1024)
            values = [raw[part][row, :, pl.ds(offset, 1024)].astype(F32) for row in rows]
            planar = [v[:1] for v in values] + [v[1:] for v in values]
            own[:, pl.ds(pl.multiple_of(part * STEP + offset, 1024), 1024)] = jnp.concatenate(planar, axis=0).astype(BF16)

        if place == steps - 1:
            pl.semaphore_wait(barrier, n_tm + 1)
            for earlier in order[: place + 1]:
                send(earlier)
        elif place >= steps:
            send(part)

    diag_acc[...] = jnp.zeros_like(diag_acc)
    low_acc[...] = jnp.zeros_like(low_acc)
    high_acc[...] = jnp.zeros_like(high_acc)

    @pl.loop(0, 2 * steps)
    def _(part):
        table_copy(part).wait()
        block = own[:, lanes(part)]
        diag_acc[...] += jnp.dot(
            cross_rows(block, block), table[lanes(part), :], preferred_element_type=F32
        )

    def diag_copy(k):
        return pltpu.make_async_remote_copy(
            diag_out.at[peer(k)], diag_in.at[k], diag_send.at[k], diag_recv.at[k],
            device_id=(here, peer(k)), device_id_type=MESH,
        )

    def side_copy(k):
        return pltpu.make_async_remote_copy(
            side_out.at[peer(k)], side_in.at[k], side_send.at[k], side_recv.at[k],
            device_id=(here, peer(k)), device_id_type=MESH,
        )

    diag = folded(diag_acc[...])
    for t in range(n_tm):
        diag_out[t] = diag[t * CH : (t + 1) * CH]
    for k in range(1, n_tm):
        diag_copy(k).start()

    for copy in index_copies[1:]:
        copy.wait()

    def next_tile(p, carry):
        count, kinds = carry[0], carry[1:]
        mine = owners[p] == here
        kind = 2 * (tiles[0, p] - here + 1) + tiles[1, p] - tiles[0, p]
        kinds = [
            jnp.where(mine & (count == s), kind, kinds[s]) for s in range(TILE_CAP)
        ]
        return (count + mine.astype(jnp.int32), *kinds)

    carry = (jnp.int32(0),) + (jnp.int32(-1),) * TILE_CAP
    kinds = lax.fori_loop(0, tiles.shape[1], next_tile, carry)[1:]

    @pl.loop(0, steps)
    def _(i):
        low_copy(i).wait_recv()
        low_acc[...] += jnp.dot(
            cross_rows(own[:, lanes(i)], from_right[:, lanes(i)]),
            table[lanes(i), :], preferred_element_type=F32,
        )
        high_copy(i).wait_recv()
        high_acc[...] += jnp.dot(
            cross_rows(from_left[:, lanes(i)], own[:, lanes(steps + i)]),
            table[lanes(steps + i), :], preferred_element_type=F32,
        )

    low, high = folded(low_acc[...]), folded(high_acc[...])
    for t in range(n_tm):
        side_out[t, :CH] = low[t * CH : (t + 1) * CH]
        side_out[t, CH:] = high[t * CH : (t + 1) * CH]
    for k in range(1, n_tm):
        side_copy(k).start()

    def right_copy(place):
        return pltpu.make_async_remote_copy(
            hop_out.at[place], hop_in.at[place], hop_send.at[place], hop_recv.at[place],
            device_id=right, device_id_type=MESH,
        )

    def left_copy(place):
        return pltpu.make_async_remote_copy(
            hop_out.at[place], hop_in.at[place], hop_send.at[place], hop_recv.at[place],
            device_id=left, device_id_type=MESH,
        )

    diag_sum = diag_out[window]
    for k in range(1, n_tm):
        diag_copy(k).wait_recv()
        diag_sum += diag_in[k]
    hop_out[0] = diag_sum
    right_copy(0).start()

    side_sum = side_out[window]
    for k in range(1, n_tm):
        side_copy(k).wait_recv()
        side_sum += side_in[k]
    hop_out[1] = side_sum[:CH]
    hop_out[2] = side_sum[CH:]
    right_copy(1).start()
    left_copy(2).start()

    right_copy(0).wait_recv()
    right_copy(1).wait_recv()
    left_copy(2).wait_recv()
    stacked = [hop_in[0], side_sum[CH:] + hop_in[1], diag_sum, side_sum[:CH] + hop_in[2]]
    lane = lax.broadcasted_iota(jnp.int32, (CH, HALF), 1)
    mirror = lax.rem(HALF - lane, HALF)
    for s in range(TILE_CAP):
        value = jnp.zeros((CH, LAGS), F32)
        for kind, tile in enumerate(stacked):
            value = jnp.where(kinds[s] == kind, tile, value)
        even, odd = value[:, :HALF], value[:, HALF:]
        before = jnp.where(lane == 0, odd, even - odd)
        before = jnp.take_along_axis(before, mirror, axis=1)
        after = jnp.where(lane == 0, even, even + odd)
        out[s] = jnp.concatenate([before, after], axis=1) * norm_scale

    for i in range(steps):
        low_copy(i).wait_send()
        high_copy(i).wait_send()
    for k in range(1, n_tm):
        diag_copy(k).wait_send()
        side_copy(k).wait_send()
    right_copy(0).wait_send()
    right_copy(1).wait_send()
    left_copy(2).wait_send()


def on_device(n_pairs, n_tm, spectra, channel_slot, tile_list, tile_owner):
    bins = spectra.shape[3]
    steps = bins // 2 // STEP
    dma = pltpu.SemaphoreType.DMA
    vmem = pl.BlockSpec(memory_space=pltpu.VMEM)
    hbm = pl.BlockSpec(memory_space=pl.ANY)
    return pl.pallas_call(
        functools.partial(kernel, n_pairs, n_tm, 1.0 / math.sqrt(2.0 * bins * n_tm)),
        out_shape=jax.ShapeDtypeStruct((TILE_CAP, CH, LAGS), F32),
        in_specs=[hbm] * 5,
        out_specs=vmem,
        scratch_shapes=[
            pltpu.SMEM(channel_slot.shape, jnp.int32),
            pltpu.SMEM(tile_list.shape[::-1], jnp.int32),
            pltpu.SMEM(tile_owner.shape, jnp.int32),
            [pltpu.VMEM((CH, 2, STEP), BF16) for _ in range(2 * steps)],
            pltpu.VMEM((2 * CH, bins), BF16),
            pltpu.VMEM((2 * CH, bins // 2), BF16),
            pltpu.VMEM((2 * CH, bins // 2), BF16),
            pltpu.VMEM((bins, LAGS), BF16),
            pltpu.VMEM((2 * CH * CH, LAGS), F32),
            pltpu.VMEM((2 * CH * CH, LAGS), F32),
            pltpu.VMEM((2 * CH * CH, LAGS), F32),
            pltpu.VMEM((n_tm, CH, LAGS), F32),
            pltpu.VMEM((n_tm, CH, LAGS), F32),
            pltpu.VMEM((n_tm, 2 * CH, LAGS), F32),
            pltpu.VMEM((n_tm, 2 * CH, LAGS), F32),
            pltpu.VMEM((3, CH, LAGS), F32),
            pltpu.VMEM((3, CH, LAGS), F32),
            dma((3,)),
            dma((2 * steps,)),
            dma((2 * steps,)),
            dma((2 * steps,)),
            dma((2 * steps,)),
            dma((n_tm,)),
            dma((n_tm,)),
            dma((n_tm,)),
            dma((n_tm,)),
            dma((3,)),
            dma((3,)),
        ],
        compiler_params=pltpu.CompilerParams(
            collective_id=0, has_side_effects=True, vmem_limit_bytes=63 * 1024 * 1024
        ),
    )(spectra[0], channel_slot, tile_list.T, tile_owner, jnp.asarray(lag_table(bins)))


def solution(mesh):
    placed = (P("tm", "pairs", None, None), P("pairs"), P(), P())
    body = functools.partial(on_device, mesh.shape["pairs"], mesh.shape["tm"])
    return jax.shard_map(
        body, mesh=mesh, in_specs=placed, out_specs=P("pairs", "tm", None), check_vma=False
    )
```

time: 381 us -> 36.5 us (0.10)
  the two profiles are of different devices: /device:TPU:24 before, /device:TPU:1 now
where the time goes in v1:
time: 36.5 us; the launch traced here: 36.4 us
  Pallas kernels  35 us (96%)
  local copies, waits for them, and re-layouts  1.38 us (4%)
    pallas_call x1, Pallas kernels, on_device(): pl.pallas_call(functools.partial(kernel, n_pairs, n_tm, 1.0 / math.sqrt(2...  35 us
    unnamed x1, local copies, waits for them, and re-layouts  1.38 us

profile of v1, /device:TPU:1, one launch (start us, length us, event | category | flops | bytes accessed | tf_op | source)
XLA Modules:
  0.0 36.4 jit_solution(324887030380474939)
XLA Ops:
  0.0 35.0 %shard_map.55 = f32[4,8,256]{2,1,0:T(8,128)} custom-call(bf16[8,2,32768]{2,1,0:T(2,128)(2,1)} %bitcast.2, s32[8]{0:T(128)} %slot_hbm.1, s32[2,63]{1,0:T(2,128)} %bitcast.3, s32[63]{0:T(128)} %owners_hbm.1, bf16[32768,256]{1,0:T(8,128)(2,1)} %constant.2.clone.table_hbm), custom_call_target="tpu_custom_call" | custom-call | tf_op jit(solution)/shard_map/pallas_call | solution.py:288
  35.0 1.4 %copy.7 = f32[4,8,256]{2,1,0:T(8,128)} copy(f32[4,8,256]{2,1,0:T(8,128)} %shard_map.55) | data formatting | bytes 65536

commit v2 on v1

--- a/solution.py
+++ b/solution.py
@@ -73,7 +73,7 @@
     out,
     slot, tiles, owners, raw, own, from_right, from_left, table,
     diag_acc, low_acc, high_acc,
-    diag_out, diag_in, side_out, side_in, hop_out, hop_in,
+    diag_out, diag_in, side_out, side_in, hop_out, hop_in, mixed,
     index_sem, raw_sem, table_sem, send_sem, recv_sem, diag_send, diag_recv,
     side_send, side_recv, hop_send, hop_recv,
 ):
@@ -84,13 +84,27 @@
     window = lax.axis_index("tm")
     right = (lax.rem(here + 1, n_pairs), window)
     left = (lax.rem(here + n_pairs - 1, n_pairs), window)
+    has_right = here < n_pairs - 1
+    has_left = here > 0
 
     def peer(k):
         return lax.rem(window + k, n_tm)
 
     barrier = pltpu.get_barrier_semaphore()
-    for device in [right, left] + [(here, peer(k)) for k in range(1, n_tm)]:
+
+    def greet(device):
         pl.semaphore_signal(barrier, inc=1, device_id=device, device_id_type=MESH)
+
+    @pl.when(has_right)
+    def _():
+        greet(right)
+
+    @pl.when(has_left)
+    def _():
+        greet(left)
+
+    for k in range(1, n_tm):
+        greet((here, peer(k)))
 
     def lanes(index):
         return pl.ds(pl.multiple_of(index * STEP, STEP), STEP)
@@ -136,9 +150,16 @@
 
     def send(part):
         if part < steps:
-            low_copy(part).start()
+
+            @pl.when(has_left)
+            def _():
+                low_copy(part).start()
+
         else:
-            high_copy(part - steps).start()
+
+            @pl.when(has_right)
+            def _():
+                high_copy(part - steps).start()
 
     index_copies[0].wait()
     rows = [slot[c] for c in range(CH)]
@@ -153,7 +174,8 @@
             own[:, pl.ds(pl.multiple_of(part * STEP + offset, 1024), 1024)] = jnp.concatenate(planar, axis=0).astype(BF16)
 
         if place == steps - 1:
-            pl.semaphore_wait(barrier, n_tm + 1)
+            beside = lax.min(here, 1) + lax.min(n_pairs - 1 - here, 1)
+            pl.semaphore_wait(barrier, n_tm - 1 + beside)
             for earlier in order[: place + 1]:
                 send(earlier)
         elif place >= steps:
@@ -204,19 +226,30 @@
     carry = (jnp.int32(0),) + (jnp.int32(-1),) * TILE_CAP
     kinds = lax.fori_loop(0, tiles.shape[1], next_tile, carry)[1:]
 
-    @pl.loop(0, steps)
-    def _(i):
+    def low_step(i):
         low_copy(i).wait_recv()
         low_acc[...] += jnp.dot(
             cross_rows(own[:, lanes(i)], from_right[:, lanes(i)]),
             table[lanes(i), :], preferred_element_type=F32,
         )
+
+    def high_step(i):
         high_copy(i).wait_recv()
         high_acc[...] += jnp.dot(
             cross_rows(from_left[:, lanes(i)], own[:, lanes(steps + i)]),
             table[lanes(steps + i), :], preferred_element_type=F32,
         )
 
+    @pl.loop(0, steps)
+    def _(i):
+        @pl.when(has_right)
+        def _():
+            low_step(i)
+
+        @pl.when(has_left)
+        def _():
+            high_step(i)
+
     low, high = folded(low_acc[...]), folded(high_acc[...])
     for t in range(n_tm):
         side_out[t, :CH] = low[t * CH : (t + 1) * CH]
@@ -241,7 +274,10 @@
         diag_copy(k).wait_recv()
         diag_sum += diag_in[k]
     hop_out[0] = diag_sum
-    right_copy(0).start()
+
+    @pl.when(has_right)
+    def _():
+        right_copy(0).start()
 
     side_sum = side_out[window]
     for k in range(1, n_tm):
@@ -249,34 +285,64 @@
         side_sum += side_in[k]
     hop_out[1] = side_sum[:CH]
     hop_out[2] = side_sum[CH:]
-    right_copy(1).start()
-    left_copy(2).start()
-
-    right_copy(0).wait_recv()
-    right_copy(1).wait_recv()
-    left_copy(2).wait_recv()
-    stacked = [hop_in[0], side_sum[CH:] + hop_in[1], diag_sum, side_sum[:CH] + hop_in[2]]
+
+    @pl.when(has_right)
+    def _():
+        right_copy(1).start()
+
+    @pl.when(here > 1)
+    def _():
+        left_copy(2).start()
+
+    def chosen(s, kind, tile):
+        return jnp.where(kinds[s] == kind, tile, 0.0)
+
+    for s in range(TILE_CAP):
+        mixed[s] = (
+            chosen(s, 1, side_sum[CH:]) + chosen(s, 2, diag_sum) + chosen(s, 3, side_sum[:CH])
+        )
+
+    @pl.when(has_left)
+    def _():
+        right_copy(0).wait_recv()
+        right_copy(1).wait_recv()
+        for s in range(TILE_CAP):
+            mixed[s] += chosen(s, 0, hop_in[0]) + chosen(s, 1, hop_in[1])
+
+    @pl.when(has_left & has_right)
+    def _():
+        left_copy(2).wait_recv()
+        for s in range(TILE_CAP):
+            mixed[s] += chosen(s, 3, hop_in[2])
+
     lane = lax.broadcasted_iota(jnp.int32, (CH, HALF), 1)
     mirror = lax.rem(HALF - lane, HALF)
     for s in range(TILE_CAP):
-        value = jnp.zeros((CH, LAGS), F32)
-        for kind, tile in enumerate(stacked):
-            value = jnp.where(kinds[s] == kind, tile, value)
-        even, odd = value[:, :HALF], value[:, HALF:]
+        even, odd = mixed[s, :, :HALF], mixed[s, :, HALF:]
         before = jnp.where(lane == 0, odd, even - odd)
         before = jnp.take_along_axis(before, mirror, axis=1)
         after = jnp.where(lane == 0, even, even + odd)
         out[s] = jnp.concatenate([before, after], axis=1) * norm_scale
 
-    for i in range(steps):
-        low_copy(i).wait_send()
-        high_copy(i).wait_send()
+    @pl.when(has_left)
+    def _():
+        for i in range(steps):
+            low_copy(i).wait_send()
+
+    @pl.when(has_right)
+    def _():
+        for i in range(steps):
+            high_copy(i).wait_send()
+        right_copy(0).wait_send()
+        right_copy(1).wait_send()
+
+    @pl.when(here > 1)
+    def _():
+        left_copy(2).wait_send()
+
     for k in range(1, n_tm):
         diag_copy(k).wait_send()
         side_copy(k).wait_send()
-    right_copy(0).wait_send()
-    right_copy(1).wait_send()
-    left_copy(2).wait_send()
 
 
 def on_device(n_pairs, n_tm, spectra, channel_slot, tile_list, tile_owner):
@@ -308,6 +374,7 @@
             pltpu.VMEM((n_tm, 2 * CH, LAGS), F32),
             pltpu.VMEM((3, CH, LAGS), F32),
             pltpu.VMEM((3, CH, LAGS), F32),
+            pltpu.VMEM((TILE_CAP, CH, LAGS), F32),
             dma((3,)),
             dma((2 * steps,)),
             dma((2 * steps,)),

time: 36.5 us -> 32.5 us (0.89)
  the two profiles are of different devices: /device:TPU:1 before, /device:TPU:24 now
where the time goes in v2:
time: 32.5 us; the launch traced here: 32.4 us
  Pallas kernels  31 us (95%)
  local copies, waits for them, and re-layouts  1.38 us (4%)
    pallas_call x1, Pallas kernels, on_device(): pl.pallas_call(functools.partial(kernel, n_pairs, n_tm, 1.0 / math.sqrt(2...  31 us
    unnamed x1, local copies, waits for them, and re-layouts  1.38 us

profile of v2, /device:TPU:24, one launch (start us, length us, event | category | flops | bytes accessed | tf_op | source)
XLA Modules:
  0.0 32.4 jit_solution(15053940188667766546)
XLA Ops:
  0.0 31.0 %shard_map.55 = f32[4,8,256]{2,1,0:T(8,128)} custom-call(bf16[8,2,32768]{2,1,0:T(2,128)(2,1)} %bitcast.2, s32[8]{0:T(128)} %slot_hbm.1, s32[2,63]{1,0:T(2,128)} %bitcast.3, s32[63]{0:T(128)} %owners_hbm.1, bf16[32768,256]{1,0:T(8,128)(2,1)} %constant.2.clone.table_hbm), custom_call_target="tpu_custom_call" | custom-call | tf_op jit(solution)/shard_map/pallas_call | solution.py:354
  31.0 1.4 %copy.7 = f32[4,8,256]{2,1,0:T(8,128)} copy(f32[4,8,256]{2,1,0:T(8,128)} %shard_map.55) | data formatting | bytes 65536

commit v3 on v1

v3 whole, which is shorter than its diff:
```python
import functools
import math

import jax
import jax.numpy as jnp
import ml_dtypes
import numpy as np
from jax import lax
from jax.experimental import pallas as pl
from jax.experimental.pallas import tpu as pltpu
from jax.sharding import PartitionSpec as P

LAGS = 256
TILE_CAP = 4
CH = 8
HALF = LAGS // 2
TURN = 512
SHIFT = TURN // 4
STEP = 4096
MESH = pl.DeviceIdType.MESH
F32 = jnp.float32
BF16 = jnp.bfloat16


def lag_table(bins):
    bin_ids = np.arange(bins)
    turn_start = bin_ids // TURN * TURN
    moved = turn_start + (bin_ids - turn_start + SHIFT) % TURN

    def phase(ids, lags):
        steps = (ids[:, None] * lags[None, :]) % (2 * bins)
        return (steps.astype(np.float32) * np.float32(math.pi / bins)).astype(np.float64)

    cosine = np.cos(phase(bin_ids, np.arange(HALF)))
    sine = -np.sin(phase(moved, np.arange(HALF)))
    sine[:, :1] = np.cos(phase(bin_ids, np.array([HALF])))
    joined = np.concatenate([cosine, sine], axis=1)
    return joined.astype(np.float32).astype(ml_dtypes.bfloat16)


def moved_on(block):
    parts = []
    for start in range(0, block.shape[1], TURN):
        parts.append(block[:, start + SHIFT : start + TURN])
        parts.append(block[:, start : start + SHIFT])
    return jnp.concatenate(parts, axis=1)


def cross_rows(lead, tail):
    lead = lead.astype(F32)
    tail = tail.astype(F32)
    tail_re, tail_im = tail[:CH], tail[CH:]
    real, imag = [], []
    for a in range(CH):
        lead_re, lead_im = lead[a : a + 1], lead[CH + a : CH + a + 1]
        real.append(lead_re * tail_re + lead_im * tail_im)
        imag.append(lead_im * tail_re - lead_re * tail_im)
    real = jnp.concatenate(real, axis=0).astype(BF16)
    imag = jnp.concatenate(imag, axis=0).astype(BF16)
    return jnp.concatenate([real, moved_on(imag)], axis=0)


def folded(acc):
    real, imag = acc[: CH * CH, :], acc[CH * CH :, :]
    lane = lax.broadcasted_iota(jnp.int32, (CH * CH, HALF), 1)
    right = imag[:, HALF:] + jnp.where(lane == 0, real[:, HALF:], 0.0)
    return jnp.concatenate([real[:, :HALF], right], axis=1)


def kernel(
    n_pairs, n_tm, norm_scale,
    spectra, slot_hbm, tiles_hbm, owners_hbm, table_hbm,
    out,
    slot, tiles, owners, raw, own, beside, table,
    diag_acc, side_acc, diag_out, diag_in, hop_out, hop_in,
    side_out, arrived, mixed,
    index_sem, raw_sem, table_sem, send_sem, recv_sem, diag_send, diag_recv,
    hop_send, hop_recv, own_send, near_send, arrived_sem,
):
    bins = own.shape[1]
    steps = bins // STEP
    here = lax.axis_index("pairs")
    window = lax.axis_index("tm")
    odd = lax.rem(window, 2)
    even_window = odd == 0
    right = lax.rem(here + 1, n_pairs)
    left = lax.rem(here + n_pairs - 1, n_pairs)
    near = lax.rem(here + 1 - 2 * odd + n_pairs, n_pairs)
    away = lax.rem(here - 1 + 2 * odd + n_pairs, n_pairs)
    to_right = lax.min(n_pairs - 1 - here, 1)
    to_left = lax.min(here, 1)
    has_right = to_right == 1
    has_left = to_left == 1
    to_near = to_right * (1 - odd) + to_left * odd
    to_away = to_left * (1 - odd) + to_right * odd
    has_near = to_near == 1
    has_away = to_away == 1
    gives_own = has_left
    gives_near = has_near & (here * odd != 1)

    def peer(k):
        return lax.rem(window + k, n_tm)

    barrier = pltpu.get_barrier_semaphore()

    def greet(block, t):
        pl.semaphore_signal(barrier, inc=1, device_id=(block, t), device_id_type=MESH)

    @pl.when(has_right)
    def _():
        for t in range(1, n_tm, 2):
            greet(right, t)

        @pl.when(even_window)
        def _():
            greet(right, window)

    @pl.when(has_left)
    def _():
        for t in range(0, n_tm, 2):
            greet(left, t)

        @pl.when(odd == 1)
        def _():
            greet(left, window)

    for k in range(1, n_tm):
        greet(here, peer(k))

    def lanes(index):
        return pl.ds(pl.multiple_of(index * STEP, STEP), STEP)

    def raw_copy(part):
        return pltpu.make_async_copy(
            spectra.at[:, :, lanes(part)], raw[part], raw_sem.at[part]
        )

    def table_copy(part):
        return pltpu.make_async_copy(
            table_hbm.at[lanes(part), :], table.at[lanes(part), :], table_sem.at[part]
        )

    index_copies = [
        pltpu.make_async_copy(source, target, index_sem.at[place])
        for place, (source, target) in enumerate(
            [(slot_hbm, slot), (tiles_hbm, tiles), (owners_hbm, owners)]
        )
    ]
    index_copies[0].start()
    for part in range(steps):
        raw_copy(part).start()
    for copy in index_copies[1:]:
        copy.start()
    def block_copy(span, place):
        return pltpu.make_async_remote_copy(
            own.at[:, span], beside.at[:, span], send_sem.at[0], recv_sem.at[place],
            device_id=(away, window), device_id_type=MESH,
        )

    last = [
        (pl.ds((steps - 1) * STEP + i * STEP // 2, STEP // 2), steps - 1 + i) for i in range(2)
    ]

    index_copies[0].wait()
    rows = [slot[c] for c in range(CH)]
    entered = 1
    for part in range(steps):
        raw_copy(part).wait()

        @pl.loop(0, STEP // 1024)
        def _(piece, part=part):
            offset = pl.multiple_of(piece * 1024, 1024)
            values = [raw[part][row, :, pl.ds(offset, 1024)].astype(F32) for row in rows]
            planar = [v[:1] for v in values] + [v[1:] for v in values]
            own[:, pl.ds(pl.multiple_of(part * STEP + offset, 1024), 1024)] = jnp.concatenate(
                planar, axis=0
            ).astype(BF16)

        if part == entered:
            pl.semaphore_wait(barrier, n_tm - 1 + n_tm * to_near + to_away)
        if part >= entered:

            @pl.when(has_away)
            def _(part=part):
                for ready in range(0 if part == entered else part, part + 1):
                    pieces = last if ready == steps - 1 else [(lanes(ready), ready)]
                    for span, place in pieces:
                        block_copy(span, place).start()

    for part in range(steps):
        table_copy(part).start()

    diag_acc[...] = jnp.zeros_like(diag_acc)
    side_acc[...] = jnp.zeros_like(side_acc)

    @pl.loop(0, steps)
    def _(part):
        table_copy(part).wait()
        block = own[:, lanes(part)]
        diag_acc[...] += jnp.dot(
            cross_rows(block, block), table[lanes(part), :], preferred_element_type=F32
        )

    def diag_copy(k):
        return pltpu.make_async_remote_copy(
            diag_out.at[peer(k)], diag_in.at[k - 1], diag_send.at[0], diag_recv.at[0],
            device_id=(here, peer(k)), device_id_type=MESH,
        )

    diag_all = pltpu.make_async_remote_copy(
        diag_out.at[pl.ds(0, n_tm - 1)], diag_in, diag_send.at[0], diag_recv.at[0],
        device_id=(here, peer(1)), device_id_type=MESH,
    )
    far_first = sorted(range(1, n_tm), key=lambda k: abs(k - n_tm // 2))

    diag = folded(diag_acc[...])
    for t in range(n_tm):
        diag_out[t] = diag[t * CH : (t + 1) * CH]
    for k in far_first:
        diag_copy(k).start()

    for copy in index_copies[1:]:
        copy.wait()

    def next_tile(p, carry):
        count, kinds = carry[0], carry[1:]
        mine = owners[p] == here
        kind = 2 * (tiles[0, p] - here + 1) + tiles[1, p] - tiles[0, p]
        kinds = [
            jnp.where(mine & (count == s), kind, kinds[s]) for s in range(TILE_CAP)
        ]
        return (count + mine.astype(jnp.int32), *kinds)

    carry = (jnp.int32(0),) + (jnp.int32(-1),) * TILE_CAP
    kinds = lax.fori_loop(0, tiles.shape[1], next_tile, carry)[1:]

    def chosen(s, kind, tile):
        return jnp.where(kinds[s] == kind, tile, 0.0)

    def side_step(span, place):
        block_copy(span, place).wait_recv()
        mine = own[:, span].astype(F32)
        other = beside[:, span].astype(F32)
        lead = jnp.where(even_window, mine, other)
        tail = jnp.where(even_window, other, mine)
        side_acc[...] += jnp.dot(
            cross_rows(lead, tail), table[span, :], preferred_element_type=F32
        )

    hop = pltpu.make_async_remote_copy(
        hop_out, hop_in, hop_send.at[0], hop_recv.at[0],
        device_id=(right, window), device_id_type=MESH,
    )

    @pl.loop(0, steps - 2)
    def _(part):
        @pl.when(has_near)
        def _():
            side_step(lanes(part), part)

    diag_all.wait_recv()
    diag_sum = diag_out[window]
    for k in range(n_tm - 1):
        diag_sum += diag_in[k]
    hop_out[...] = diag_sum

    @pl.when(has_right)
    def _():
        hop.start()

    @pl.when(has_near)
    def _():
        side_step(lanes(steps - 2), steps - 2)
        for span, place in last:
            side_step(span, place)

    def own_copy(k):
        return pltpu.make_async_remote_copy(
            side_out.at[peer(k)], arrived.at[window], own_send.at[0], arrived_sem.at[0],
            device_id=(here, peer(k)), device_id_type=MESH,
        )

    def right_copy(k):
        return pltpu.make_async_remote_copy(
            side_out.at[peer(k)], arrived.at[n_tm + window // 2],
            near_send.at[0], arrived_sem.at[0],
            device_id=(right, peer(k)), device_id_type=MESH,
        )

    def left_copy(k):
        return pltpu.make_async_remote_copy(
            side_out.at[peer(k)], arrived.at[n_tm + n_tm // 2 + window // 2],
            near_send.at[0], arrived_sem.at[0],
            device_id=(left, peer(k)), device_id_type=MESH,
        )

    def several(buffer, count, send):
        return pltpu.make_async_remote_copy(
            buffer.at[pl.ds(0, count)], buffer.at[pl.ds(0, count)], send, arrived_sem.at[0],
            device_id=(right, window), device_id_type=MESH,
        )

    side = folded(side_acc[...])
    for t in range(n_tm):
        side_out[t] = side[t * CH : (t + 1) * CH]

    @pl.when(gives_near)
    def _():
        @pl.when(even_window)
        def _():
            for k in far_first + [0]:
                right_copy(k).start()

        @pl.when(odd == 1)
        def _():
            for k in far_first + [0]:
                left_copy(k).start()

    @pl.when(gives_own)
    def _():
        for k in far_first:
            own_copy(k).start()

    arrived[window] = side_out[window]
    for s in range(TILE_CAP):
        mixed[s] = chosen(s, 2, diag_sum)

    @pl.when(has_away)
    def _():
        pltpu.make_async_remote_copy(
            own, beside, send_sem.at[0], recv_sem.at[0],
            device_id=(away, window), device_id_type=MESH,
        ).wait_send()

    diag_all.wait_send()

    @pl.when(has_right)
    def _():
        hop.wait_send()

    @pl.when(has_left)
    def _():
        hop.wait_recv()
        for s in range(TILE_CAP):
            mixed[s] += chosen(s, 0, hop_in[...])

    @pl.when(has_left & has_right)
    def _():
        several(arrived, 2 * n_tm - 1, own_send.at[0]).wait_recv()
        after = arrived[0]
        for place in range(2, n_tm, 2):
            after += arrived[place]
        for place in range(n_tm + n_tm // 2, 2 * n_tm):
            after += arrived[place]
        for s in range(TILE_CAP):
            mixed[s] += chosen(s, 3, after)

    @pl.when(has_left & (to_right == 0))
    def _():
        several(arrived, n_tm - 1 + n_tm // 2, own_send.at[0]).wait_recv()

    @pl.when(has_left)
    def _():
        before = arrived[1]
        for place in range(3, n_tm, 2):
            before += arrived[place]
        for place in range(n_tm, n_tm + n_tm // 2):
            before += arrived[place]
        for s in range(TILE_CAP):
            mixed[s] += chosen(s, 1, before)

    lane = lax.broadcasted_iota(jnp.int32, (CH, HALF), 1)
    mirror = lax.rem(HALF - lane, HALF)
    for s in range(TILE_CAP):
        cosine, sine = mixed[s, :, :HALF], mixed[s, :, HALF:]
        before = jnp.where(lane == 0, sine, cosine - sine)
        before = jnp.take_along_axis(before, mirror, axis=1)
        after = jnp.where(lane == 0, cosine, cosine + sine)
        out[s] = jnp.concatenate([before, after], axis=1) * norm_scale

    @pl.when(gives_near)
    def _():
        several(arrived, n_tm, near_send.at[0]).wait_send()

    @pl.when(gives_own)
    def _():
        several(arrived, n_tm - 1, own_send.at[0]).wait_send()


def on_device(n_pairs, n_tm, spectra, channel_slot, tile_list, tile_owner):
    bins = spectra.shape[3]
    steps = bins // STEP
    dma = pltpu.SemaphoreType.DMA
    vmem = pl.BlockSpec(memory_space=pltpu.VMEM)
    hbm = pl.BlockSpec(memory_space=pl.ANY)
    group = pltpu.VMEM((n_tm, CH, LAGS), F32)
    share = pltpu.VMEM((CH, LAGS), F32)
    return pl.pallas_call(
        functools.partial(kernel, n_pairs, n_tm, 1.0 / math.sqrt(2.0 * bins * n_tm)),
        out_shape=jax.ShapeDtypeStruct((TILE_CAP, CH, LAGS), F32),
        in_specs=[hbm] * 5,
        out_specs=vmem,
        scratch_shapes=[
            pltpu.SMEM(channel_slot.shape, jnp.int32),
            pltpu.SMEM(tile_list.shape[::-1], jnp.int32),
            pltpu.SMEM(tile_owner.shape, jnp.int32),
            [pltpu.VMEM((CH, 2, STEP), BF16) for _ in range(steps)],
            pltpu.VMEM((2 * CH, bins), BF16),
            pltpu.VMEM((2 * CH, bins), BF16),
            pltpu.VMEM((bins, LAGS), BF16),
            pltpu.VMEM((2 * CH * CH, LAGS), F32),
            pltpu.VMEM((2 * CH * CH, LAGS), F32),
            group,
            pltpu.VMEM((n_tm - 1, CH, LAGS), F32),
            share,
            share,
            group,
            pltpu.VMEM((2 * n_tm, CH, LAGS), F32),
            pltpu.VMEM((TILE_CAP, CH, LAGS), F32),
            dma((3,)),
            dma((steps,)),
            dma((steps,)),
            dma((1,)),
            dma((steps + 1,)),
            dma((1,)),
            dma((1,)),
            dma((1,)),
            dma((1,)),
            dma((1,)),
            dma((1,)),
            dma((1,)),
        ],
        compiler_params=pltpu.CompilerParams(
            collective_id=0, has_side_effects=True, vmem_limit_bytes=63 * 1024 * 1024
        ),
    )(spectra[0], channel_slot, tile_list.T, tile_owner, jnp.asarray(lag_table(bins)))


def solution(mesh):
    placed = (P("tm", "pairs", None, None), P("pairs"), P(), P())
    body = functools.partial(on_device, mesh.shape["pairs"], mesh.shape["tm"])
    return jax.shard_map(
        body, mesh=mesh, in_specs=placed, out_specs=P("pairs", "tm", None), check_vma=False
    )
```

time: 36.5 us -> 30.3 us (0.83)
  the two profiles are of different devices: /device:TPU:1 before, /device:TPU:24 now
where the time goes in v3:
time: 30.3 us; the launch traced here: 30 us
  Pallas kernels  28.6 us (94%)
  local copies, waits for them, and re-layouts  1.38 us (5%)
    pallas_call x1, Pallas kernels, on_device(): pl.pallas_call(functools.partial(kernel, n_pairs, n_tm, 1.0 / math.sqrt(2...  28.6 us
    unnamed x1, local copies, waits for them, and re-layouts  1.38 us

profile of v3, /device:TPU:24, one launch (start us, length us, event | category | flops | bytes accessed | tf_op | source)
XLA Modules:
  0.0 30.0 jit_solution(6602090491286886929)
XLA Ops:
  0.0 28.6 %shard_map.55 = f32[4,8,256]{2,1,0:T(8,128)} custom-call(bf16[8,2,32768]{2,1,0:T(2,128)(2,1)} %bitcast.2, s32[8]{0:T(128)} %slot_hbm.1, s32[2,63]{1,0:T(2,128)} %bitcast.3, s32[63]{0:T(128)} %owners_hbm.1, bf16[32768,256]{1,0:T(8,128)(2,1)} %constant.2.clone.table_hbm), custom_call_target="tpu_custom_call" | custom-call | tf_op jit(solution)/shard_map/pallas_call | solution.py:398
  28.6 1.4 %copy.7 = f32[4,8,256]{2,1,0:T(8,128)} copy(f32[4,8,256]{2,1,0:T(8,128)} %shard_map.55) | data formatting | bytes 65536

commit v4 on v3

--- a/solution.py
+++ b/solution.py
@@ -17,6 +17,9 @@
 TURN = 512
 SHIFT = TURN // 4
 STEP = 4096
+PIECE = STEP // 2
+ROW = 8
+MOVED = 2 * PIECE
 MESH = pl.DeviceIdType.MESH
 F32 = jnp.float32
 BF16 = jnp.bfloat16
@@ -73,9 +76,9 @@
     out,
     slot, tiles, owners, raw, own, beside, table,
     diag_acc, side_acc, diag_out, diag_in, hop_out, hop_in,
-    side_out, arrived, mixed,
+    side_out, arrived, mixed, moved_lead, moved_tail,
     index_sem, raw_sem, table_sem, send_sem, recv_sem, diag_send, diag_recv,
-    hop_send, hop_recv, own_send, near_send, arrived_sem,
+    hop_send, hop_recv, own_send, near_send, arrived_sem, moved_send, moved_recv,
 ):
     bins = own.shape[1]
     steps = bins // STEP
@@ -96,6 +99,11 @@
     has_near = to_near == 1
     has_away = to_away == 1
     gives_own = has_left
+    starts_row = to_left * (1 - lax.min(lax.rem(here, ROW), 1))
+    ends_row = to_right * (1 - lax.min(ROW - 1 - lax.rem(here, ROW), 1))
+    gives_tail = starts_row * (1 - odd) == 1
+    gives_lead = ends_row * (1 - odd) == 1
+    takes_moved = starts_row * odd == 1
     gives_near = has_near & (here * odd != 1)
 
     def peer(k):
@@ -108,23 +116,18 @@
 
     @pl.when(has_right)
     def _():
-        for t in range(1, n_tm, 2):
-            greet(right, t)
-
-        @pl.when(even_window)
-        def _():
-            greet(right, window)
+        greet(right, window)
 
     @pl.when(has_left)
     def _():
-        for t in range(0, n_tm, 2):
-            greet(left, t)
-
-        @pl.when(odd == 1)
-        def _():
-            greet(left, window)
-
-    for k in range(1, n_tm):
+        greet(left, window)
+
+    @pl.when(takes_moved)
+    def _():
+        greet(left, window - 1)
+
+    far_first = sorted(range(1, n_tm), key=lambda k: abs(k - n_tm // 2))
+    for k in far_first:
         greet(here, peer(k))
 
     def lanes(index):
@@ -157,9 +160,20 @@
             device_id=(away, window), device_id_type=MESH,
         )
 
-    last = [
-        (pl.ds((steps - 1) * STEP + i * STEP // 2, STEP // 2), steps - 1 + i) for i in range(2)
+    kept = bins - MOVED
+    pieces = [
+        (pl.ds(start, PIECE), steps - 2 + i)
+        for i, start in enumerate(range(bins - 2 * STEP, bins, PIECE))
     ]
+    moved_span = pl.ds(kept, MOVED)
+    tail_copy = pltpu.make_async_remote_copy(
+        own.at[:, moved_span], moved_tail, moved_send.at[0], moved_recv.at[0],
+        device_id=(here, lax.rem(window + 1, n_tm)), device_id_type=MESH,
+    )
+    lead_copy = pltpu.make_async_remote_copy(
+        own.at[:, moved_span], moved_lead, moved_send.at[0], moved_recv.at[1],
+        device_id=(right, lax.rem(window + 1, n_tm)), device_id_type=MESH,
+    )
 
     index_copies[0].wait()
     rows = [slot[c] for c in range(CH)]
@@ -177,15 +191,31 @@
             ).astype(BF16)
 
         if part == entered:
-            pl.semaphore_wait(barrier, n_tm - 1 + n_tm * to_near + to_away)
-        if part >= entered:
+            pl.semaphore_wait(
+                barrier, n_tm - 1 + to_left + to_right + ends_row * (1 - odd)
+            )
+        if entered <= part < steps - 2:
 
             @pl.when(has_away)
             def _(part=part):
                 for ready in range(0 if part == entered else part, part + 1):
-                    pieces = last if ready == steps - 1 else [(lanes(ready), ready)]
-                    for span, place in pieces:
-                        block_copy(span, place).start()
+                    block_copy(lanes(ready), ready).start()
+
+        if part >= steps - 2:
+            for span, place in pieces[2 * (part - steps + 2) :][:2]:
+                needed = has_away if span.start < kept else has_away & ~gives_tail
+
+                @pl.when(needed)
+                def _(span=span, place=place):
+                    block_copy(span, place).start()
+
+    @pl.when(gives_tail)
+    def _():
+        tail_copy.start()
+
+    @pl.when(gives_lead)
+    def _():
+        lead_copy.start()
 
     for part in range(steps):
         table_copy(part).start()
@@ -211,8 +241,6 @@
         diag_out.at[pl.ds(0, n_tm - 1)], diag_in, diag_send.at[0], diag_recv.at[0],
         device_id=(here, peer(1)), device_id_type=MESH,
     )
-    far_first = sorted(range(1, n_tm), key=lambda k: abs(k - n_tm // 2))
-
     diag = folded(diag_acc[...])
     for t in range(n_tm):
         diag_out[t] = diag[t * CH : (t + 1) * CH]
@@ -237,14 +265,17 @@
     def chosen(s, kind, tile):
         return jnp.where(kinds[s] == kind, tile, 0.0)
 
+    def side_sum(lead, tail, span):
+        side_acc[...] += jnp.dot(
+            cross_rows(lead, tail), table[span, :], preferred_element_type=F32
+        )
+
     def side_step(span, place):
         block_copy(span, place).wait_recv()
         mine = own[:, span].astype(F32)
         other = beside[:, span].astype(F32)
-        lead = jnp.where(even_window, mine, other)
-        tail = jnp.where(even_window, other, mine)
-        side_acc[...] += jnp.dot(
-            cross_rows(lead, tail), table[span, :], preferred_element_type=F32
+        side_sum(
+            jnp.where(even_window, mine, other), jnp.where(even_window, other, mine), span
         )
 
     hop = pltpu.make_async_remote_copy(
@@ -268,10 +299,19 @@
     def _():
         hop.start()
 
-    @pl.when(has_near)
-    def _():
-        side_step(lanes(steps - 2), steps - 2)
-        for span, place in last:
+    @pl.when(takes_moved)
+    def _():
+        tail_copy.wait_recv()
+        lead_copy.wait_recv()
+        for start in range(0, MOVED, PIECE):
+            part = pl.ds(start, PIECE)
+            side_sum(moved_lead[:, part], moved_tail[:, part], pl.ds(kept + start, PIECE))
+
+    for span, place in pieces:
+        needed = has_near if span.start < kept else has_near & ~gives_lead
+
+        @pl.when(needed)
+        def _(span=span, place=place):
             side_step(span, place)
 
     def own_copy(k):
@@ -325,12 +365,24 @@
     for s in range(TILE_CAP):
         mixed[s] = chosen(s, 2, diag_sum)
 
-    @pl.when(has_away)
-    def _():
+    def sent(span):
         pltpu.make_async_remote_copy(
-            own, beside, send_sem.at[0], recv_sem.at[0],
+            own.at[:, span], beside.at[:, span], send_sem.at[0], recv_sem.at[0],
             device_id=(away, window), device_id_type=MESH,
         ).wait_send()
+
+    @pl.when(has_away & ~gives_tail)
+    def _():
+        sent(pl.ds(0, bins))
+
+    @pl.when(gives_tail)
+    def _():
+        sent(pl.ds(0, kept))
+        tail_copy.wait_send()
+
+    @pl.when(gives_lead)
+    def _():
+        lead_copy.wait_send()
 
     diag_all.wait_send()
 
@@ -417,18 +469,22 @@
             group,
             pltpu.VMEM((2 * n_tm, CH, LAGS), F32),
             pltpu.VMEM((TILE_CAP, CH, LAGS), F32),
+            pltpu.VMEM((2 * CH, MOVED), BF16),
+            pltpu.VMEM((2 * CH, MOVED), BF16),
             dma((3,)),
             dma((steps,)),
             dma((steps,)),
             dma((1,)),
-            dma((steps + 1,)),
-            dma((1,)),
-            dma((1,)),
-            dma((1,)),
-            dma((1,)),
-            dma((1,)),
-            dma((1,)),
-            dma((1,)),
+            dma((steps + 2,)),
+            dma((1,)),
+            dma((1,)),
+            dma((1,)),
+            dma((1,)),
+            dma((1,)),
+            dma((1,)),
+            dma((1,)),
+            dma((1,)),
+            dma((2,)),
         ],
         compiler_params=pltpu.CompilerParams(
             collective_id=0, has_side_effects=True, vmem_limit_bytes=63 * 1024 * 1024

time: 30.3 us -> 28.9 us (0.954)
  Pallas kernels: 28.6 us -> 27.2 us
    pallas_call x1, Pallas kernels: 28.6 us -> 27.2 us  [on_device(): pl.pallas_call(functools.partial(kernel, n_pairs, n_tm, 1.0 / math.sqrt(2...]
where the time goes in v4:
time: 28.9 us; the launch traced here: 28.6 us
  Pallas kernels  27.2 us (94%)
  local copies, waits for them, and re-layouts  1.38 us (5%)
    pallas_call x1, Pallas kernels, on_device(): pl.pallas_call(functools.partial(kernel, n_pairs, n_tm, 1.0 / math.sqrt(2...  27.2 us
    unnamed x1, local copies, waits for them, and re-layouts  1.38 us

profile of v4, /device:TPU:24, one launch (start us, length us, event | category | flops | bytes accessed | tf_op | source)
XLA Modules:
  0.0 28.6 jit_solution(4495152823249627921)
XLA Ops:
  0.0 27.2 %shard_map.55 = f32[4,8,256]{2,1,0:T(8,128)} custom-call(bf16[8,2,32768]{2,1,0:T(2,128)(2,1)} %bitcast.2, s32[8]{0:T(128)} %slot_hbm.1, s32[2,63]{1,0:T(2,128)} %bitcast.3, s32[63]{0:T(128)} %owners_hbm.1, bf16[32768,256]{1,0:T(8,128)(2,1)} %constant.2.clone.table_hbm), custom_call_target="tpu_custom_call" | custom-call | tf_op jit(solution)/shard_map/pallas_call | solution.py:450
  27.2 1.4 %copy.7 = f32[4,8,256]{2,1,0:T(8,128)} copy(f32[4,8,256]{2,1,0:T(8,128)} %shard_map.55) | data formatting | bytes 65536

commit v5 on v4

--- a/solution.py
+++ b/solution.py
@@ -487,9 +487,16 @@
             dma((2,)),
         ],
         compiler_params=pltpu.CompilerParams(
-            collective_id=0, has_side_effects=True, vmem_limit_bytes=63 * 1024 * 1024
+            collective_id=0, has_side_effects=True, vmem_limit_bytes=48 * 1024 * 1024
         ),
-    )(spectra[0], channel_slot, tile_list.T, tile_owner, jnp.asarray(lag_table(bins)))
+    )(
+        *(
+            pltpu.with_memory_space_constraint(operand, pltpu.HBM)
+            for operand in (
+                spectra[0], channel_slot, tile_list.T, tile_owner, jnp.asarray(lag_table(bins))
+            )
+        )
+    )
 
 
 def solution(mesh):

time: 28.9 us -> 27.5 us (0.952)
  local copies, waits for them, and re-layouts: 1.38 us -> 0.62 us
  Pallas kernels: 27.2 us -> 26.6 us
    unnamed x1, local copies, waits for them, and re-layouts: 1.38 us -> 0.62 us
    pallas_call x1, Pallas kernels: 27.2 us -> 26.6 us  [on_device(): pl.pallas_call(functools.partial(kernel, n_pairs, n_tm, 1.0 / math.sqrt(2...]
where the time goes in v5:
time: 27.5 us; the launch traced here: 27.2 us
  Pallas kernels  26.6 us (97%)
  local copies, waits for them, and re-layouts  0.62 us (2%)
    pallas_call x1, Pallas kernels, on_device(): pl.pallas_call(functools.partial(kernel, n_pairs, n_tm, 1.0 / math.sqrt(2...  26.6 us
    unnamed x1, local copies, waits for them, and re-layouts  0.62 us

profile of v5, /device:TPU:24, one launch (start us, length us, event | category | flops | bytes accessed | tf_op | source)
XLA Modules:
  0.0 27.2 jit_solution(45250099882687379)
XLA Ops:
  0.0 26.6 %shard_map.55 = f32[4,8,256]{2,1,0:T(8,128)S(1)} custom-call(bf16[8,2,32768]{2,1,0:T(2,128)(2,1)} %bitcast.2, s32[8]{0:T(128)} %slot_hbm.1, s32[2,63]{1,0:T(2,128)} %bitcast.3, s32[63]{0:T(128)} %owners_hbm.1, bf16[32768,256]{1,0:T(8,128)(2,1)} %constant.2.clone.table_hbm), custom_call_target="tpu_custom_call" | custom-call | tf_op jit(solution)/shard_map/pallas_call | solution.py:450
  26.6 0.6 %copy.7 = f32[4,8,256]{2,1,0:T(8,128)} copy(f32[4,8,256]{2,1,0:T(8,128)S(1)} %shard_map.55) | data formatting | bytes 65536

commit v6 on v3

--- a/solution.py
+++ b/solution.py
@@ -75,13 +75,13 @@
     diag_acc, side_acc, diag_out, diag_in, hop_out, hop_in,
     side_out, arrived, mixed,
     index_sem, raw_sem, table_sem, send_sem, recv_sem, diag_send, diag_recv,
-    hop_send, hop_recv, own_send, near_send, arrived_sem,
+    hop_send, hop_recv, own_send, near_send, arrived_sem, ready,
 ):
     bins = own.shape[1]
     steps = bins // STEP
     here = lax.axis_index("pairs")
     window = lax.axis_index("tm")
-    odd = lax.rem(window, 2)
+    odd = 1 - lax.rem(window, 2)
     even_window = odd == 0
     right = lax.rem(here + 1, n_pairs)
     left = lax.rem(here + n_pairs - 1, n_pairs)
@@ -106,26 +106,18 @@
     def greet(block, t):
         pl.semaphore_signal(barrier, inc=1, device_id=(block, t), device_id_type=MESH)
 
-    @pl.when(has_right)
-    def _():
-        for t in range(1, n_tm, 2):
-            greet(right, t)
-
-        @pl.when(even_window)
-        def _():
-            greet(right, window)
-
-    @pl.when(has_left)
-    def _():
-        for t in range(0, n_tm, 2):
-            greet(left, t)
-
-        @pl.when(odd == 1)
-        def _():
-            greet(left, window)
-
-    for k in range(1, n_tm):
-        greet(here, peer(k))
+    @pl.when(has_near)
+    def _():
+        greet(near, window)
+
+    far_first = sorted(range(1, n_tm), key=lambda k: abs(k - n_tm // 2))
+    core = lax.rem(window, 2)
+    first = window - core
+    others = [lax.rem(first + 2 * dx + n_tm, n_tm) for dx in (-1, 1)]
+    for base in others:
+        for t in range(2):
+            greet(here, base + t)
+    greet(here, first + 1 - core)
 
     def lanes(index):
         return pl.ds(pl.multiple_of(index * STEP, STEP), STEP)
@@ -177,15 +169,23 @@
             ).astype(BF16)
 
         if part == entered:
-            pl.semaphore_wait(barrier, n_tm - 1 + n_tm * to_near + to_away)
-        if part >= entered:
+            pl.semaphore_wait(barrier, 5 + to_away)
+            pl.semaphore_signal(
+                ready, inc=1, device_id=(here, others[0] + core), device_id_type=MESH
+            )
+        if entered <= part < steps - 1:
 
             @pl.when(has_away)
             def _(part=part):
-                for ready in range(0 if part == entered else part, part + 1):
-                    pieces = last if ready == steps - 1 else [(lanes(ready), ready)]
-                    for span, place in pieces:
-                        block_copy(span, place).start()
+                for sent in range(0 if part == entered else part, part + 1):
+                    block_copy(lanes(sent), sent).start()
+
+    pl.semaphore_wait(ready, 1)
+
+    @pl.when(has_away)
+    def _():
+        for span, place in last:
+            block_copy(span, place).start()
 
     for part in range(steps):
         table_copy(part).start()
@@ -211,8 +211,6 @@
         diag_out.at[pl.ds(0, n_tm - 1)], diag_in, diag_send.at[0], diag_recv.at[0],
         device_id=(here, peer(1)), device_id_type=MESH,
     )
-    far_first = sorted(range(1, n_tm), key=lambda k: abs(k - n_tm // 2))
-
     diag = folded(diag_acc[...])
     for t in range(n_tm):
         diag_out[t] = diag[t * CH : (t + 1) * CH]
@@ -347,8 +345,8 @@
     @pl.when(has_left & has_right)
     def _():
         several(arrived, 2 * n_tm - 1, own_send.at[0]).wait_recv()
-        after = arrived[0]
-        for place in range(2, n_tm, 2):
+        after = arrived[1]
+        for place in range(3, n_tm, 2):
             after += arrived[place]
         for place in range(n_tm + n_tm // 2, 2 * n_tm):
             after += arrived[place]
@@ -361,8 +359,8 @@
 
     @pl.when(has_left)
     def _():
-        before = arrived[1]
-        for place in range(3, n_tm, 2):
+        before = arrived[0]
+        for place in range(2, n_tm, 2):
             before += arrived[place]
         for place in range(n_tm, n_tm + n_tm // 2):
             before += arrived[place]
@@ -429,11 +427,19 @@
             dma((1,)),
             dma((1,)),
             dma((1,)),
+            pltpu.SemaphoreType.REGULAR,
         ],
         compiler_params=pltpu.CompilerParams(
-            collective_id=0, has_side_effects=True, vmem_limit_bytes=63 * 1024 * 1024
+            collective_id=0, has_side_effects=True, vmem_limit_bytes=48 * 1024 * 1024
         ),
-    )(spectra[0], channel_slot, tile_list.T, tile_owner, jnp.asarray(lag_table(bins)))
+    )(
+        *(
+            pltpu.with_memory_space_constraint(operand, pltpu.HBM)
+            for operand in (
+                spectra[0], channel_slot, tile_list.T, tile_owner, jnp.asarray(lag_table(bins))
+            )
+        )
+    )
 
 
 def solution(mesh):

time: 30.3 us -> 26.9 us (0.89)
  Pallas kernels: 28.6 us -> 26.2 us
  local copies, waits for them, and re-layouts: 1.38 us -> 0.62 us
    pallas_call x1, Pallas kernels: 28.6 us -> 26.2 us  [on_device(): pl.pallas_call(functools.partial(kernel, n_pairs, n_tm, 1.0 / math.sqrt(2...]
    unnamed x1, local copies, waits for them, and re-layouts: 1.38 us -> 0.62 us
where the time goes in v6:
time: 26.9 us; the launch traced here: 26.8 us
  Pallas kernels  26.2 us (97%)
  local copies, waits for them, and re-layouts  0.62 us (2%)
    pallas_call x1, Pallas kernels, on_device(): pl.pallas_call(functools.partial(kernel, n_pairs, n_tm, 1.0 / math.sqrt(2...  26.2 us
    unnamed x1, local copies, waits for them, and re-layouts  0.62 us

profile of v6, /device:TPU:24, one launch (start us, length us, event | category | flops | bytes accessed | tf_op | source)
XLA Modules:
  0.0 26.8 jit_solution(14264061997326511042)
XLA Ops:
  0.0 26.2 %shard_map.55 = f32[4,8,256]{2,1,0:T(8,128)S(1)} custom-call(bf16[8,2,32768]{2,1,0:T(2,128)(2,1)} %bitcast.2, s32[8]{0:T(128)} %slot_hbm.1, s32[2,63]{1,0:T(2,128)} %bitcast.3, s32[63]{0:T(128)} %owners_hbm.1, bf16[32768,256]{1,0:T(8,128)(2,1)} %constant.2.clone.table_hbm), custom_call_target="tpu_custom_call" | custom-call | tf_op jit(solution)/shard_map/pallas_call | solution.py:396
  26.2 0.6 %copy.7 = f32[4,8,256]{2,1,0:T(8,128)} copy(f32[4,8,256]{2,1,0:T(8,128)S(1)} %shard_map.55) | data formatting | bytes 65536

commit v7 on v6

--- a/solution.py
+++ b/solution.py
@@ -17,6 +17,7 @@
 TURN = 512
 SHIFT = TURN // 4
 STEP = 4096
+PIECE = STEP // 4
 MESH = pl.DeviceIdType.MESH
 F32 = jnp.float32
 BF16 = jnp.bfloat16
@@ -110,14 +111,21 @@
     def _():
         greet(near, window)
 
+    core = lax.rem(window, 2)
+    partner = window + 1 - 2 * core
+    beside_odd = [lax.rem(window - core + 2 * dx + n_tm, n_tm) + 1 for dx in (-1, 1)]
     far_first = sorted(range(1, n_tm), key=lambda k: abs(k - n_tm // 2))
-    core = lax.rem(window, 2)
-    first = window - core
-    others = [lax.rem(first + 2 * dx + n_tm, n_tm) for dx in (-1, 1)]
-    for base in others:
-        for t in range(2):
-            greet(here, base + t)
-    greet(here, first + 1 - core)
+    greet(here, partner)
+
+    @pl.when(core == 1)
+    def _():
+        for t in beside_odd:
+            greet(here, t)
+
+    def vouch(place, t):
+        pl.semaphore_signal(
+            ready.at[place], inc=1, device_id=(here, t), device_id_type=MESH
+        )
 
     def lanes(index):
         return pl.ds(pl.multiple_of(index * STEP, STEP), STEP)
@@ -150,14 +158,32 @@
         )
 
     last = [
-        (pl.ds((steps - 1) * STEP + i * STEP // 2, STEP // 2), steps - 1 + i) for i in range(2)
+        (pl.ds((steps - 1) * STEP + i * PIECE, PIECE), steps - 1 + i)
+        for i in range(STEP // PIECE)
     ]
+
+    def slot_kinds():
+        for copy in index_copies[1:]:
+            copy.wait()
+
+        def next_tile(p, carry):
+            count, kinds = carry[0], carry[1:]
+            mine = owners[p] == here
+            kind = 2 * (tiles[0, p] - here + 1) + tiles[1, p] - tiles[0, p]
+            kinds = [
+                jnp.where(mine & (count == s), kind, kinds[s]) for s in range(TILE_CAP)
+            ]
+            return (count + mine.astype(jnp.int32), *kinds)
+
+        carry = (jnp.int32(0),) + (jnp.int32(-1),) * TILE_CAP
+        return lax.fori_loop(0, tiles.shape[1], next_tile, carry)[1:]
 
     index_copies[0].wait()
     rows = [slot[c] for c in range(CH)]
     entered = 1
     for part in range(steps):
-        raw_copy(part).wait()
+        if part <= entered:
+            raw_copy(part).wait()
 
         @pl.loop(0, STEP // 1024)
         def _(piece, part=part):
@@ -169,10 +195,13 @@
             ).astype(BF16)
 
         if part == entered:
-            pl.semaphore_wait(barrier, 5 + to_away)
-            pl.semaphore_signal(
-                ready, inc=1, device_id=(here, others[0] + core), device_id_type=MESH
-            )
+            pl.semaphore_wait(barrier, 1 + 2 * core + to_away)
+
+            @pl.when(core == 1)
+            def _():
+                for t in beside_odd:
+                    vouch(0, t)
+
         if entered <= part < steps - 1:
 
             @pl.when(has_away)
@@ -180,15 +209,16 @@
                 for sent in range(0 if part == entered else part, part + 1):
                     block_copy(lanes(sent), sent).start()
 
-    pl.semaphore_wait(ready, 1)
-
-    @pl.when(has_away)
-    def _():
-        for span, place in last:
-            block_copy(span, place).start()
-
-    for part in range(steps):
-        table_copy(part).start()
+        if part == entered:
+            for later in range(entered + 1, steps):
+                raw_copy(later).wait()
+            for later in range(steps):
+                table_copy(later).start()
+
+    @pl.when(core == 1)
+    def _():
+        pl.semaphore_wait(ready.at[0], 2)
+        vouch(1, beside_odd[0])
 
     diag_acc[...] = jnp.zeros_like(diag_acc)
     side_acc[...] = jnp.zeros_like(side_acc)
@@ -200,6 +230,20 @@
         diag_acc[...] += jnp.dot(
             cross_rows(block, block), table[lanes(part), :], preferred_element_type=F32
         )
+
+    @pl.when(core == 1)
+    def _():
+        pl.semaphore_wait(ready.at[1], 1)
+        vouch(2, partner)
+
+    @pl.when(core == 0)
+    def _():
+        pl.semaphore_wait(ready.at[2], 1)
+
+    @pl.when(has_away)
+    def _():
+        for span, place in last:
+            block_copy(span, place).start()
 
     def diag_copy(k):
         return pltpu.make_async_remote_copy(
@@ -217,20 +261,7 @@
     for k in far_first:
         diag_copy(k).start()
 
-    for copy in index_copies[1:]:
-        copy.wait()
-
-    def next_tile(p, carry):
-        count, kinds = carry[0], carry[1:]
-        mine = owners[p] == here
-        kind = 2 * (tiles[0, p] - here + 1) + tiles[1, p] - tiles[0, p]
-        kinds = [
-            jnp.where(mine & (count == s), kind, kinds[s]) for s in range(TILE_CAP)
-        ]
-        return (count + mine.astype(jnp.int32), *kinds)
-
-    carry = (jnp.int32(0),) + (jnp.int32(-1),) * TILE_CAP
-    kinds = lax.fori_loop(0, tiles.shape[1], next_tile, carry)[1:]
+    kinds = slot_kinds()
 
     def chosen(s, kind, tile):
         return jnp.where(kinds[s] == kind, tile, 0.0)
@@ -419,15 +450,15 @@
             dma((steps,)),
             dma((steps,)),
             dma((1,)),
-            dma((steps + 1,)),
-            dma((1,)),
-            dma((1,)),
-            dma((1,)),
-            dma((1,)),
-            dma((1,)),
-            dma((1,)),
-            dma((1,)),
-            pltpu.SemaphoreType.REGULAR,
+            dma((steps - 1 + STEP // PIECE,)),
+            dma((1,)),
+            dma((1,)),
+            dma((1,)),
+            dma((1,)),
+            dma((1,)),
+            dma((1,)),
+            dma((1,)),
+            pltpu.SemaphoreType.REGULAR((3,)),
         ],
         compiler_params=pltpu.CompilerParams(
             collective_id=0, has_side_effects=True, vmem_limit_bytes=48 * 1024 * 1024

time: 26.9 us -> 26.8 us (level)
  no operation moved by 1% of the time
where the time goes in v7:
time: 26.8 us; the launch traced here: 26.7 us
  Pallas kernels  26.1 us (97%)
  local copies, waits for them, and re-layouts  0.62 us (2%)
    pallas_call x1, Pallas kernels, on_device(): pl.pallas_call(functools.partial(kernel, n_pairs, n_tm, 1.0 / math.sqrt(2...  26.1 us
    unnamed x1, local copies, waits for them, and re-layouts  0.62 us

profile of v7, /device:TPU:24, one launch (start us, length us, event | category | flops | bytes accessed | tf_op | source)
XLA Modules:
  0.0 26.7 jit_solution(231530647558115713)
XLA Ops:
  0.0 26.1 %shard_map.55 = f32[4,8,256]{2,1,0:T(8,128)S(1)} custom-call(bf16[8,2,32768]{2,1,0:T(2,128)(2,1)} %bitcast.2, s32[8]{0:T(128)} %slot_hbm.1, s32[2,63]{1,0:T(2,128)} %bitcast.3, s32[63]{0:T(128)} %owners_hbm.1, bf16[32768,256]{1,0:T(8,128)(2,1)} %constant.2.clone.table_hbm), custom_call_target="tpu_custom_call" | custom-call | tf_op jit(solution)/shard_map/pallas_call | solution.py:427
  26.1 0.6 %copy.7 = f32[4,8,256]{2,1,0:T(8,128)} copy(f32[4,8,256]{2,1,0:T(8,128)S(1)} %shard_map.55) | data formatting | bytes 65536

commit v8 on v7

--- a/solution.py
+++ b/solution.py
@@ -17,7 +17,7 @@
 TURN = 512
 SHIFT = TURN // 4
 STEP = 4096
-PIECE = STEP // 4
+PIECES = ((0, 2048), (2048, 1024), (3072, 512), (3584, 512))
 MESH = pl.DeviceIdType.MESH
 F32 = jnp.float32
 BF16 = jnp.bfloat16
@@ -158,8 +158,8 @@
         )
 
     last = [
-        (pl.ds((steps - 1) * STEP + i * PIECE, PIECE), steps - 1 + i)
-        for i in range(STEP // PIECE)
+        (pl.ds((steps - 1) * STEP + start, size), steps - 1 + i)
+        for i, (start, size) in enumerate(PIECES)
     ]
 
     def slot_kinds():
@@ -180,7 +180,7 @@
 
     index_copies[0].wait()
     rows = [slot[c] for c in range(CH)]
-    entered = 1
+    entered = 0
     for part in range(steps):
         if part <= entered:
             raw_copy(part).wait()
@@ -450,7 +450,7 @@
             dma((steps,)),
             dma((steps,)),
             dma((1,)),
-            dma((steps - 1 + STEP // PIECE,)),
+            dma((steps - 1 + len(PIECES),)),
             dma((1,)),
             dma((1,)),
             dma((1,)),

time: 26.8 us -> 26.7 us (level)
  no operation moved by 1% of the time
where the time goes in v8:
time: 26.7 us; the launch traced here: 26.6 us
  Pallas kernels  26 us (97%)
  local copies, waits for them, and re-layouts  0.62 us (2%)
    pallas_call x1, Pallas kernels, on_device(): pl.pallas_call(functools.partial(kernel, n_pairs, n_tm, 1.0 / math.sqrt(2...  26 us
    unnamed x1, local copies, waits for them, and re-layouts  0.62 us

profile of v8, /device:TPU:24, one launch (start us, length us, event | category | flops | bytes accessed | tf_op | source)
XLA Modules:
  0.0 26.6 jit_solution(1467503058032834162)
XLA Ops:
  0.0 26.0 %shard_map.55 = f32[4,8,256]{2,1,0:T(8,128)S(1)} custom-call(bf16[8,2,32768]{2,1,0:T(2,128)(2,1)} %bitcast.2, s32[8]{0:T(128)} %slot_hbm.1, s32[2,63]{1,0:T(2,128)} %bitcast.3, s32[63]{0:T(128)} %owners_hbm.1, bf16[32768,256]{1,0:T(8,128)(2,1)} %constant.2.clone.table_hbm), custom_call_target="tpu_custom_call" | custom-call | tf_op jit(solution)/shard_map/pallas_call | solution.py:427
  26.0 0.6 %copy.7 = f32[4,8,256]{2,1,0:T(8,128)} copy(f32[4,8,256]{2,1,0:T(8,128)S(1)} %shard_map.55) | data formatting | bytes 65536

commit v9 on v8

--- a/solution.py
+++ b/solution.py
@@ -196,20 +196,19 @@
 
         if part == entered:
             pl.semaphore_wait(barrier, 1 + 2 * core + to_away)
-
+        if entered <= part < steps - 1:
+
+            @pl.when(has_away)
+            def _(part=part):
+                for sent in range(0 if part == entered else part, part + 1):
+                    block_copy(lanes(sent), sent).start()
+
+        if part == entered:
             @pl.when(core == 1)
             def _():
                 for t in beside_odd:
                     vouch(0, t)
 
-        if entered <= part < steps - 1:
-
-            @pl.when(has_away)
-            def _(part=part):
-                for sent in range(0 if part == entered else part, part + 1):
-                    block_copy(lanes(sent), sent).start()
-
-        if part == entered:
             for later in range(entered + 1, steps):
                 raw_copy(later).wait()
             for later in range(steps):

time: 26.7 us -> 26.7 us (level)
  no operation moved by 1% of the time
where the time goes in v9:
time: 26.7 us; the launch traced here: 26.6 us
  Pallas kernels  26 us (97%)
  local copies, waits for them, and re-layouts  0.62 us (2%)
    pallas_call x1, Pallas kernels, on_device(): pl.pallas_call(functools.partial(kernel, n_pairs, n_tm, 1.0 / math.sqrt(2...  26 us
    unnamed x1, local copies, waits for them, and re-layouts  0.62 us

profile of v9, /device:TPU:24, one launch (start us, length us, event | category | flops | bytes accessed | tf_op | source)
XLA Modules:
  0.0 26.6 jit_solution(18266098901517152921)
XLA Ops:
  0.0 26.0 %shard_map.55 = f32[4,8,256]{2,1,0:T(8,128)S(1)} custom-call(bf16[8,2,32768]{2,1,0:T(2,128)(2,1)} %bitcast.2, s32[8]{0:T(128)} %slot_hbm.1, s32[2,63]{1,0:T(2,128)} %bitcast.3, s32[63]{0:T(128)} %owners_hbm.1, bf16[32768,256]{1,0:T(8,128)(2,1)} %constant.2.clone.table_hbm), custom_call_target="tpu_custom_call" | custom-call | tf_op jit(solution)/shard_map/pallas_call | solution.py:426
  26.0 0.6 %copy.7 = f32[4,8,256]{2,1,0:T(8,128)} copy(f32[4,8,256]{2,1,0:T(8,128)S(1)} %shard_map.55) | data formatting | bytes 65536
